TPU v7x, 128 devices: a whole 4x4x4 slice. The times are simulated.
128 devices in a mesh: blk: 16 (over x, z), ma: 8 (over y, core).
Axes of the slice: x: 4, y: 4, z: 4, core: 2. Of those that a mesh axis runs over, the one named last changes fastest.
Arguments:
- weights: bfloat16 [128, 128, 8, 4, 128], P(('blk', 'ma')), may hold values from 0.099609375 to 0.3984375
- offsets: int32 [128, 128, 8, 128], P(('blk', 'ma')), may hold values from 0 to 127
- counts: int32 [128, 128], P(('blk', 'ma')), may hold values from 1 to 8, 576 in all within a row
- block_ids: int32 [128, 128, 8], P(('blk', 'ma')), may hold values from 0 to 127
- m_table: int32 [1536], replicated, may hold values from 0 to 1535, as said below
- legendre: bfloat16 [1536, 1664, 512], P(('blk', 'ma')), as said below
Outputs:
- kappa_band: float32 [4, 512, 4096], P(None, ('blk', 'ma'))
- potential: float32 [4, 512, 4096], P(None, ('blk', 'ma'))
Inputs may be any that keep to these rules, and one draw needn't show every extreme that they name: Groups with index below counts[d, e] are live, the others hold no particles; each row sums to (8 + 1) * 128 // 2 and reaches 8. `m_table`: a permutation of 0 to 1535. legendre[j, l, q] is zero for every l below m_table[j].
All inputs are finite; a program needn't handle non-finite values.
Results may differ from a plain program's by a relative error of at most 0.0058.
Values may be sent and summed in bfloat16 or wider, within the bound.
A program may use at most 128 MiB of HBM per device.

v0:
```python
import math

import jax
import jax.numpy as jnp
from jax import lax
from jax.sharding import PartitionSpec as P

NPHI = 4096


highest = lax.Precision.HIGHEST


def split_length(length):
    factor = 1
    for candidate in range(1, math.isqrt(length) + 1):
        if length % candidate == 0:
            factor = candidate
    return (factor, length // factor)


def phase_table(row_count, col_count, period):
    row_index = lax.broadcasted_iota(jnp.int32, (row_count, col_count), 0)
    col_index = lax.broadcasted_iota(jnp.int32, (row_count, col_count), 1)
    angles = (row_index * col_index % period).astype(jnp.float32) * (2.0 * jnp.pi / period)
    return (jnp.cos(angles), jnp.sin(angles))


def forward_dft(signal, length):
    first, second = split_length(length)
    row_count = signal.shape[0]
    cube = signal.reshape(row_count, first, second)
    cos_first, sin_first = phase_table(first, first, first)
    section_real = jnp.einsum("rks,km->rms", cube, cos_first, precision=highest)
    section_imag = -jnp.einsum("rks,km->rms", cube, sin_first, precision=highest)
    twist_c, twist_s = phase_table(first, second, length)
    turned_real = section_real * twist_c + section_imag * twist_s
    turned_imag = section_imag * twist_c - section_real * twist_s
    cos_second, sin_second = phase_table(second, second, second)
    out_real = jnp.einsum("rms,sn->rnm", turned_real, cos_second, precision=highest) + jnp.einsum(
        "rms,sn->rnm", turned_imag, sin_second, precision=highest
    )
    out_imag = jnp.einsum("rms,sn->rnm", turned_imag, cos_second, precision=highest) - jnp.einsum(
        "rms,sn->rnm", turned_real, sin_second, precision=highest
    )
    return (out_real.reshape(row_count, length), out_imag.reshape(row_count, length))


def inverse_real(spec_real, spec_imag, length):
    first, second = split_length(length)
    row_count = spec_real.shape[0]
    grid_real = spec_real.reshape(row_count, second, first)
    grid_imag = spec_imag.reshape(row_count, second, first)
    cos_second, sin_second = phase_table(second, second, second)
    section_real = jnp.einsum("rnm,ns->rms", grid_real, cos_second, precision=highest) - jnp.einsum(
        "rnm,ns->rms", grid_imag, sin_second, precision=highest
    )
    section_imag = jnp.einsum("rnm,ns->rms", grid_imag, cos_second, precision=highest) + jnp.einsum(
        "rnm,ns->rms", grid_real, sin_second, precision=highest
    )
    twist_c, twist_s = phase_table(first, second, length)
    turned_real = section_real * twist_c - section_imag * twist_s
    turned_imag = section_real * twist_s + section_imag * twist_c
    cos_first, sin_first = phase_table(first, first, first)
    result = jnp.einsum("rms,mk->rks", turned_real, cos_first, precision=highest) - jnp.einsum(
        "rms,mk->rks", turned_imag, sin_first, precision=highest
    )
    return result.reshape(row_count, length)


def per_device(weights, offsets, counts, block_ids, m_table, legendre):
    band_count = lax.axis_size("blk")
    mode_groups = lax.axis_size("ma")
    devices = band_count * mode_groups
    device = lax.axis_index("blk") * mode_groups + lax.axis_index("ma")
    groups = weights[0]
    capacity = groups.shape[1]
    bin_count = groups.shape[2]
    cycle_length = NPHI
    cycles_here = legendre.shape[2] // devices
    blocks_here = cycles_here * cycle_length // 128
    slots_here = legendre.shape[0]
    live_mask = lax.broadcasted_iota(jnp.int32, (devices, capacity), 1) < counts[0][:, None]
    columns = lax.broadcasted_iota(jnp.int32, (1, 1, 1, 128), 3)
    onehot = (offsets[0][:, :, :, None] == columns).astype(jnp.bfloat16)
    partial_value = jnp.einsum(
        "dcbs,dcsp->dcbp", groups, onehot, preferred_element_type=jnp.float32
    )
    partial_value = jnp.where(live_mask[:, :, None, None], partial_value, 0.0)
    sent_ids = block_ids[0].astype(jnp.float32)
    arrived, arrived_ids = (
        lax.all_to_all(partial_value, ("blk", "ma"), split_axis=0, concat_axis=0, tiled=True),
        lax.all_to_all(sent_ids, ("blk", "ma"), split_axis=0, concat_axis=0, tiled=True),
    )
    received = arrived.reshape(devices * capacity, bin_count * 128)
    slot_ids = arrived_ids.reshape(devices * capacity, 1)
    selector = (slot_ids == lax.broadcasted_iota(jnp.float32, (1, blocks_here), 1)).astype(
        jnp.float32
    )
    counted = jnp.einsum("gl,gq->lq", selector, received, precision=highest)
    convergence = (
        counted.reshape(blocks_here, bin_count, 128)
        .transpose(1, 0, 2)
        .reshape(bin_count * cycles_here, cycle_length)
    )
    mode_count = m_table.shape[0]
    spectrum_real, spectrum_imag = forward_dft(convergence, cycle_length)
    real_part = jnp.take(spectrum_real, m_table, axis=1)
    imag_part = jnp.take(spectrum_imag, m_table, axis=1)
    parity = (device * cycles_here + lax.broadcasted_iota(jnp.int32, (cycles_here, 1), 0)) % 2
    twists = (m_table[None, :] * parity).astype(jnp.float32) * (jnp.pi / cycle_length)
    twist_cos = jnp.cos(twists)
    twist_sin = jnp.sin(twists)
    real_part = (real_part / cycle_length).reshape(bin_count, cycles_here, mode_count)
    imag_part = (imag_part / cycle_length).reshape(bin_count, cycles_here, mode_count)
    real_turned = real_part * twist_cos + imag_part * twist_sin
    imag_turned = imag_part * twist_cos - real_part * twist_sin
    coefficients = jnp.stack([real_turned, imag_turned], axis=2).astype(jnp.bfloat16)
    by_owner = coefficients.reshape(bin_count, cycles_here, 2, devices, slots_here)
    outgoing = by_owner.transpose(3, 4, 0, 2, 1)
    mode_rows = lax.all_to_all(outgoing, ("blk", "ma"), split_axis=0, concat_axis=4, tiled=True)[0]
    harmonic = jnp.einsum("jlr,jbcr->jbcl", legendre, mode_rows, preferred_element_type=jnp.float32)
    degrees = lax.broadcasted_iota(jnp.float32, (1, 1, 1, legendre.shape[1]), 3)
    filter_gain = jnp.where(
        degrees > 0.5, -20000.0 / jnp.maximum(degrees * (degrees + 1.0), 1.0), 0.0
    )
    filtered = jnp.stack([harmonic, harmonic * filter_gain], axis=1).astype(jnp.bfloat16)
    synthesis = jnp.einsum(
        "jlr,jfbcl->jfbcr", legendre, filtered, preferred_element_type=jnp.float32
    ).astype(jnp.bfloat16)
    outgoing_maps = synthesis.reshape(slots_here, 2, bin_count, 2, devices, cycles_here)
    mode_weight = jnp.where(m_table == 0, 1.0, 2.0).astype(jnp.float32)
    turn_cos = jnp.transpose(twist_cos)[:, None, None, :]
    turn_sin = jnp.transpose(twist_sin)[:, None, None, :]
    mode_scale = mode_weight[:, None, None, None]
    values = lax.all_to_all(outgoing_maps, ("blk", "ma"), split_axis=4, concat_axis=0, tiled=True)[
        :, :, :, :, 0, :
    ].astype(jnp.float32)
    real_in = values[:, :, :, 0, :]
    imag_in = values[:, :, :, 1, :]
    real_out = (real_in * turn_cos - imag_in * turn_sin) * mode_scale
    imag_out = (real_in * turn_sin + imag_in * turn_cos) * mode_scale
    item_count = values.shape[1]
    flat_real = jnp.transpose(real_out.reshape(mode_count, -1))
    flat_imag = jnp.transpose(imag_out.reshape(mode_count, -1))
    row_total = flat_real.shape[0]
    full_real = jnp.zeros((row_total, cycle_length), jnp.float32).at[:, m_table].set(flat_real)
    full_imag = jnp.zeros((row_total, cycle_length), jnp.float32).at[:, m_table].set(flat_imag)
    maps_out = inverse_real(full_real, full_imag, cycle_length)
    sky_maps = maps_out.reshape(item_count, bin_count, cycles_here, cycle_length)
    return (sky_maps[0], sky_maps[1])


def solution(mesh):
    placed = (
        P(("blk", "ma"), None, None, None, None),
        P(("blk", "ma"), None, None, None),
        P(("blk", "ma"), None),
        P(("blk", "ma"), None, None),
        P(),
        P(("blk", "ma"), None, None),
    )
    return jax.shard_map(
        per_device,
        mesh=mesh,
        in_specs=placed,
        out_specs=(P(None, ("blk", "ma"), None), P(None, ("blk", "ma"), None)),
        check_vma=False,
    )
```

profile of v0, /device:TPU:1, one launch (start us, length us, event | category | flops | bytes accessed | tf_op | source)
XLA Modules:
  0.0 234.8 jit_solution(16867247106737583700)
XLA Ops:
  0.6 0.9 copy.82
  2.2 11.5 %all-to-all-start = ((f32[128,1,8]{2,1,0:T(1,128)}), f32[128,1,8]{2,1,0:T(1,128)S(1)}, u32[]{:S(2)}, u32[]{:S(2)}) async-start(f32[128,1,8]{2,1,0:T(1,128)} %bitcast.1), calls=%async_computation | async-start | bytes 131072 | tf_op jit(solution)/shard_map/all_to_all | solution.py:93
  14.4 30.7 %select_bitcast_fusion = f32[128,8,4,128]{3,2,1,0:T(4,128)} fusion(s32[128,8,128]{2,1,0:T(8,128)} %bitcast.148, bf16[1,128,8,4,128]{4,3,2,1,0:T(4,128)(2,1)S(1)} %copy-done, pred[128,8]{1,0:T(8,128)(4,1)S(1)} %iota_compare_fusion.5), kind=kOutput, calls=%fused_computation.13 | convolution fusion | flops 151519232 | bytes 3671040 | tf_op jit(solution)/shard_map/dcbs,dcsp->dcbp/dot_general | solution.py:86
  45.1 9.8 %all-to-all-start.1 = ((f32[128,8,4,128]{3,2,1,0:T(4,128)}), f32[128,8,4,128]{3,2,1,0:T(4,128)S(1)}, u32[]{:S(2)}, u32[]{:S(2)}) async-start(f32[128,8,4,128]{3,2,1,0:T(4,128)} %select_bitcast_fusion), calls=%async_computation.1 | async-start | bytes 4194304 | tf_op jit(solution)/shard_map/all_to_all | solution.py:92
  60.6 24.7 %all-to-all-done.1 = f32[128,8,4,128]{3,2,1,0:T(4,128)S(1)} async-done(((f32[128,8,4,128]{3,2,1,0:T(4,128)}), f32[128,8,4,128]{3,2,1,0:T(4,128)S(1)}, u32[]{:S(2)}, u32[]{:S(2)}) %all-to-all-start.1) | async-done | bytes 2097184 | tf_op jit(solution)/shard_map/all_to_all | solution.py:92
  85.3 1.5 copy.131
  86.8 1.9 copy.83
  88.7 1.3 convolution_bitcast_fusion
  91.6 1.7 fusion.29
  93.4 2.5 %fusion.25 = f32[64,16,64]{2,0,1:T(8,128)} fusion(f32[64,16,64]{2,0,1:T(8,128)S(1)} %fusion.56, f32[64,16,64]{2,0,1:T(8,128)S(1)} %convolution_negate_fusion, f32[64,64]{1,0:T(8,128)S(1)} %copy.85, f32[64,64]{1,0:T(8,128)S(1)} %copy.84), kind=kOutput, calls=%fused_computation.42 | convolution fusion | flops 50585600 | bytes 819200 | tf_op jit(solution)/shard_map/rms,sn->rnm/dot_general | solution.py:43
  95.9 2.5 %fusion.8 = f32[16,64,64]{2,1,0:T(8,128)} fusion(f32[64,16,64]{2,0,1:T(8,128)S(1)} %fusion.29, f32[64,16,64]{2,0,1:T(8,128)S(1)} %fusion.56, f32[64,16,64]{2,0,1:T(8,128)S(1)} %convolution_negate_fusion, f32[64,64]{1,0:T(8,128)S(1)} %copy.85, f32[64,64]{1,0:T(8,128)S(1)} %copy.84), kind=kOutput, calls=%fused_computation.22 | convolution fusion | flops 50651136 | bytes 1081344 | tf_op jit(solution)/shard_map/rms,sn->rnm/dot_general | solution.py:40
  98.4 1.7 copy.120
  100.1 3.7 %gather_fusion = f32[1536,16]{1,0:T(8,128)} fusion(f32[16,4096]{0,1:T(8,128)S(1)} %bitcast.146, s32[2048]{0:T(1024)S(1)} %pad_clamp_fusion), kind=kCustom, calls=%fused_computation.clone | custom fusion | bytes 202752 | tf_op jit(solution)/shard_map/jit(_take)/gather | solution.py:108
  103.8 2.0 copy.87
  105.8 3.6 %fusion.7 = f32[16,64,64]{2,1,0:T(8,128)} fusion(f32[64,16,64]{2,0,1:T(8,128)} %fusion.25, f32[64,16,64]{2,0,1:T(8,128)S(1)} %convolution_negate_fusion, f32[64,16,64]{2,0,1:T(8,128)S(1)} %fusion.56, f32[64,64]{1,0:T(8,128)S(1)} %copy.85, f32[64,64]{1,0:T(8,128)S(1)} %copy.84), kind=kOutput, calls=%fused_computation.20 | convolution fusion | flops 50651136 | bytes 1081344 | tf_op jit(solution)/shard_map/rms,sn->rnm/dot_general | solution.py:43
  109.4 1.7 copy.121
  111.1 13.4 %gather_fusion.1 = f32[1536,16]{1,0:T(8,128)S(1)} fusion(f32[16,4096]{0,1:T(8,128)S(1)} %bitcast.145, s32[2048]{0:T(1024)S(1)} %pad_clamp_fusion), kind=kCustom, calls=%fused_computation.1.clone | custom fusion | bytes 202752 | tf_op jit(solution)/shard_map/jit(_take)/gather | solution.py:109
  124.8 1.1 reshape.341
  125.9 1.1 reshape.343
  127.1 1.2 multiply_add_fusion
  128.9 1.0 copy.95
  130.3 1.9 reshape.411
  132.2 4.5 %all-to-all-start.2 = ((bf16[128,2,192]{2,1,0:T(2,128)(2,1)}), bf16[128,2,192]{2,1,0:T(2,128)(2,1)S(1)}, u32[]{:S(2)}, u32[]{:S(2)}) async-start(bf16[128,2,192]{2,1,0:T(2,128)(2,1)} %reshape.411), calls=%async_computation.2 | async-start | bytes 262144 | tf_op jit(solution)/shard_map/all_to_all | solution.py:121
  136.7 10.1 %all-to-all-done.2 = bf16[128,2,192]{2,1,0:T(2,128)(2,1)S(1)} async-done(((bf16[128,2,192]{2,1,0:T(2,128)(2,1)}), bf16[128,2,192]{2,1,0:T(2,128)(2,1)S(1)}, u32[]{:S(2)}, u32[]{:S(2)}) %all-to-all-start.2) | async-done | bytes 98336 | tf_op jit(solution)/shard_map/all_to_all | solution.py:121
  146.8 1.3 reshape.412
  149.3 9.9 %convert_bitcast_fusion.1 = (bf16[12,1,4,2,1664]{4,2,3,0,1:T(4,128)(2,1)S(1)}, bf16[12,1,4,2,1664]{4,2,3,0,1:T(4,128)(2,1)S(1)}) fusion(f32[1664]{0:T(1024)S(1)} %fusion.87, bf16[12,4,2,512]{3,1,2,0:T(4,128)(2,1)S(1)} %copy.97, bf16[12,1664,512]{2,1,0:T(8,128)(2,1)} %param.13), kind=kOutput, calls=%fused_computation.57 | convolution fusion | flops 164057088 | bytes 21191168 | tf_op jit(solution)/shard_map/jlr,jbcr->jbcl/dot_general | solution.py:122
  159.2 10.2 %fusion.9 = bf16[12,2,4,2,512]{4,2,3,1,0:T(4,128)(2,1)S(1)} fusion(bf16[12,1664,512]{2,1,0:T(8,128)(2,1)} %param.13, bf16[12,1,4,2,1664]{4,2,3,0,1:T(4,128)(2,1)S(1)} %get-tuple-element.10, bf16[12,1,4,2,1664]{4,2,3,0,1:T(4,128)(2,1)S(1)} %get-tuple-element.9), kind=kOutput, calls=%fused_computation.23 | convolution fusion | flops 327573504 | bytes 21282816 | tf_op jit(solution)/shard_map/jlr,jfbcl->jfbcr/dot_general | solution.py:128
  169.3 1.1 copy.99
  170.4 2.5 %copy.132 = bf16[12,2,4,2,128,4]{0,5,3,2,1,4:T(4,128)(2,1)} copy(bf16[12,2,4,2,128,4]{0,5,4,3,2,1:T(4,128)(2,1)S(1)} %bitcast.142) | data formatting | bytes 393216 | tf_op jit(solution)/shard_map/reshape | solution.py:131
  173.0 5.8 %reshape.413 = bf16[128,2,384]{2,1,0:T(2,128)(2,1)} reshape(bf16[128,2,4,2,4,12]{5,4,3,2,1,0:T(4,128)(2,1)} %bitcast.143) | data formatting | bytes 393216
  178.7 4.8 %all-to-all-start.3 = ((bf16[128,2,384]{2,1,0:T(2,128)(2,1)}), bf16[128,2,384]{2,1,0:T(2,128)(2,1)S(1)}, u32[]{:S(2)}, u32[]{:S(2)}) async-start(bf16[128,2,384]{2,1,0:T(2,128)(2,1)} %reshape.413), calls=%async_computation.3 | async-start | bytes 393216 | tf_op jit(solution)/shard_map/all_to_all | solution.py:136
  183.6 10.3 %all-to-all-done.3 = bf16[128,2,384]{2,1,0:T(2,128)(2,1)S(1)} async-done(((bf16[128,2,384]{2,1,0:T(2,128)(2,1)}), bf16[128,2,384]{2,1,0:T(2,128)(2,1)S(1)}, u32[]{:S(2)}, u32[]{:S(2)}) %all-to-all-start.3) | async-done | bytes 196640 | tf_op jit(solution)/shard_map/all_to_all | solution.py:136
  193.8 4.8 %reshape.414 = bf16[128,2,4,2,4,12]{5,4,3,2,1,0:T(4,128)(2,1)S(1)} reshape(bf16[128,2,384]{2,1,0:T(2,128)(2,1)S(1)} %all-to-all-done.3) | data formatting | bytes 393216
  198.7 1.1 convert_bitcast_fusion
  199.7 4.4 %copy.101 = f32[128,12,2,4,2,1,4]{1,0,6,4,3,2,5:T(8,128)} copy(f32[128,12,2,4,2,1,4]{1,6,4,3,2,0,5:T(4,128)S(1)} %convert_bitcast_fusion) | data formatting | bytes 786432 | tf_op jit(solution)/shard_map/convert_element_type | solution.py:138
  204.1 5.4 %reshape.347 = f32[1536,2,4,2,4]{0,4,3,2,1:T(4,128)S(1)} reshape(f32[128,12,2,4,2,1,4]{1,0,6,4,3,2,5:T(8,128)} %copy.101) | data formatting | bytes 786432 | tf_op jit(solution)/shard_map/convert_element_type | solution.py:138
  210.1 5.0 %scatter_custom_fusion = f32[32,4096]{0,1:T(8,128)S(1)} fusion(s32[1536]{0:T(1024)} %copy-done.6, f32[1536,32]{1,0:T(8,128)S(1)} %copy.102, f32[]{:T(128)} %constant.82.clone.1), kind=kCustom, calls=%fused_computation.37 | custom fusion | bytes 524800 | tf_op jit(solution)/shard_map/scatter | solution.py:147
  215.0 1.5 copy.103
  216.5 1.1 fusion.51
  217.9 6.1 %scatter_custom_fusion.1 = f32[32,4096]{0,1:T(8,128)} fusion(s32[1536]{0:T(1024)} %copy-done.6, f32[1536,32]{1,0:T(8,128)S(1)} %copy.105, f32[]{:T(128)} %constant.82.clone.1), kind=kCustom, calls=%fused_computation.35 | custom fusion | bytes 524800 | tf_op jit(solution)/shard_map/scatter | solution.py:148
  224.0 2.9 %copy.106 = f32[32,64,64]{1,2,0:T(8,128)S(1)} copy(f32[32,64,64]{0,2,1:T(8,128)} %bitcast.138) | data formatting | bytes 1048576 | tf_op jit(solution)/shard_map/reshape | solution.py:53
  226.9 1.1 fusion.49
  228.1 1.1 convolution_subtract_fusion.1
  229.2 1.1 convolution_add_fusion
  230.3 1.2 fusion.16
  231.5 1.2 fusion.6
  232.8 0.9 squeeze.24
  233.7 0.9 squeeze.25
  (61 shorter events, 11.8 us)
Async XLA Ops:
  0.6 13.8 %copy-start = (bf16[1,128,8,4,128]{4,3,2,1,0:T(4,128)(2,1)S(1)}, bf16[1,128,8,4,128]{4,3,2,1,0:T(4,128)(2,1)}, u32[]{:S(2)}) copy-start(bf16[1,128,8,4,128]{4,3,2,1,0:T(4,128)(2,1)} %param.8) | copy-start | bytes 3145732
  2.2 42.9 %all-to-all-start = ((f32[128,1,8]{2,1,0:T(1,128)}), f32[128,1,8]{2,1,0:T(1,128)S(1)}, u32[]{:S(2)}, u32[]{:S(2)}) async-start(f32[128,1,8]{2,1,0:T(1,128)} %bitcast.1), calls=%async_computation | async-start | bytes 131072 | tf_op jit(solution)/shard_map/all_to_all | solution.py:93
  45.1 10.2 %copy-start.5 = (s32[1536]{0:T(1024)S(1)}, s32[1536]{0:T(1024)}, u32[]{:S(2)}) copy-start(s32[1536]{0:T(1024)} %param.12) | copy-start | bytes 18436
  45.1 40.2 %all-to-all-start.1 = ((f32[128,8,4,128]{3,2,1,0:T(4,128)}), f32[128,8,4,128]{3,2,1,0:T(4,128)S(1)}, u32[]{:S(2)}, u32[]{:S(2)}) async-start(f32[128,8,4,128]{3,2,1,0:T(4,128)} %select_bitcast_fusion), calls=%async_computation.1 | async-start | bytes 4194304 | tf_op jit(solution)/shard_map/all_to_all | solution.py:92
  58.6 0.6 copy-start.6
  109.4 15.4 %copy-start.4 = (f32[1536,16]{0,1:T(8,128)S(1)}, f32[1536,16]{0,1:T(8,128)}, u32[]{:S(2)}) copy-start(f32[1536,16]{0,1:T(8,128)} %copy.87) | copy-start | bytes 294916
  109.4 15.4 %copy-start.7 = (pred[1536]{0:T(1024)(128)(4,1)S(1)}, pred[1536]{0:T(1024)(128)(4,1)}, u32[]{:S(2)}) copy-start(pred[1536]{0:T(1024)(128)(4,1)} %compare_and_fusion) | copy-start | bytes 4612
  132.2 14.6 %all-to-all-start.2 = ((bf16[128,2,192]{2,1,0:T(2,128)(2,1)}), bf16[128,2,192]{2,1,0:T(2,128)(2,1)S(1)}, u32[]{:S(2)}, u32[]{:S(2)}) async-start(bf16[128,2,192]{2,1,0:T(2,128)(2,1)} %reshape.411), calls=%async_computation.2 | async-start | bytes 262144 | tf_op jit(solution)/shard_map/all_to_all | solution.py:121
  178.7 15.1 %all-to-all-start.3 = ((bf16[128,2,384]{2,1,0:T(2,128)(2,1)}), bf16[128,2,384]{2,1,0:T(2,128)(2,1)S(1)}, u32[]{:S(2)}, u32[]{:S(2)}) async-start(bf16[128,2,384]{2,1,0:T(2,128)(2,1)} %reshape.413), calls=%async_computation.3 | async-start | bytes 393216 | tf_op jit(solution)/shard_map/all_to_all | solution.py:136
  204.1 5.6 %copy-start.2 = (f32[1536,32]{0,1:T(8,128)S(1)}, f32[1536,32]{0,1:T(8,128)}, u32[]{:S(2)}) copy-start(f32[1536,32]{0,1:T(8,128)} %mul.407) | copy-start | bytes 589828
  204.1 5.6 %copy-start.3 = (f32[1536,32]{0,1:T(8,128)S(1)}, f32[1536,32]{0,1:T(8,128)}, u32[]{:S(2)}) copy-start(f32[1536,32]{0,1:T(8,128)} %mul.410) | copy-start | bytes 589828
  231.5 3.2 %copy-start.1 = (bf16[1,128,8,4,128]{4,3,2,1,0:T(4,128)(2,1)S(1)}, bf16[1,128,8,4,128]{4,3,2,1,0:T(4,128)(2,1)}, u32[]{:S(2)}) copy-start(bf16[1,128,8,4,128]{4,3,2,1,0:T(4,128)(2,1)} %param.8) | copy-start | bytes 3145732
where the time goes:
time: 239 us; the launch traced here: 235 us
  local copies, waits for them, and re-layouts  81.3 us (34%)
  matrix products  70.6 us (30%)
  waiting for transfers between devices  45 us (19%)
  starting transfers between devices  30.6 us (13%)
  other arithmetic  6.02 us (3%)
    dot_general x1, matrix products, per_device(): jnp.einsum('dcbs,dcsp->dcbp', groups, onehot, preferred_element_type=jnp....  30.7 us
    all_to_all x1, waiting for transfers between devices, per_device(): lax.all_to_all(partial_value, ('blk', 'ma'), split_axis=0, concat_axis=0,...  24.7 us
    unnamed x23, local copies, waits for them, and re-layouts  16.7 us
    gather x2, local copies, waits for them, and re-layouts, per_device(): imag_part = jnp.take(spectrum_imag, m_table, axis=1)  13.7 us
    all_to_all x1, starting transfers between devices, per_device(): lax.all_to_all(sent_ids, ('blk', 'ma'), split_axis=0, concat_axis=0, tile...  11.5 us
    scatter x2, local copies, waits for them, and re-layouts, per_device(): jnp.zeros((row_total, cycle_length), jnp.float32).at[:, m_table]  11 us
    all_to_all x1, waiting for transfers between devices, per_device(): lax.all_to_all(outgoing_maps, ('blk', 'ma'), split_axis=4, concat_axis=0,...  10.3 us
    dot_general x1, matrix products, per_device(): jnp.einsum('jlr,jfbcl->jfbcr', legendre, filtered, preferred_element_type...  10.2 us
  transfers between devices with their start and end apart: 4, of which 3 were waited for; matrix products, arithmetic and copies ran while one was open for 16% of the time, Pallas kernels for 0%

commit v1 on v0

v1 whole, which is shorter than its diff:
```python
import math

import jax
import jax.numpy as jnp
import numpy as np
from jax import lax
from jax.experimental import pallas as pl
from jax.experimental.pallas import tpu as pltpu
from jax.sharding import PartitionSpec as P

NPHI = 4096
BANDS = 16
LOCAL = 8
DEVICES = BANDS * LOCAL
CAP = 8
NBIN = 4
SLOTS = 12
DEGREES = 1664
CYCLES = 512
MESH_IDS = pl.DeviceIdType.MESH
bf16 = jnp.bfloat16
f32 = jnp.float32


def nn(a, b):
    return lax.dot_general(a, b, (((1,), (0,)), ((), ())), preferred_element_type=f32)


def nt(a, b):
    return lax.dot_general(a, b, (((1,), (1,)), ((), ())), preferred_element_type=f32)


def two_parts(x):
    high = x.astype(bf16)
    return high, (x - high.astype(f32)).astype(bf16)


def iota(shape, axis):
    return lax.broadcasted_iota(jnp.int32, shape, axis)


def as_one_hot(mask):
    return jnp.where(mask, 1.0, 0.0).astype(bf16)


def tables():
    import ml_dtypes

    def halves(x):
        high = x.astype(np.float32).astype(ml_dtypes.bfloat16)
        low = (x - high.astype(np.float64)).astype(np.float32).astype(ml_dtypes.bfloat16)
        return high, low

    turn = 2.0 * np.pi
    pair, par, quad = np.arange(16), np.arange(2), np.arange(4)
    kb, p, m2 = np.arange(32), np.arange(128), np.arange(64)
    m1 = 2 * pair[None, :] + par[:, None]
    keep = (m2 < 48).astype(np.float64)
    angle = turn * (m1[:, :, None] * kb % 32) / 32
    both = np.stack([np.cos(angle), -np.sin(angle)]) / NPHI
    first = np.einsum("rabk,qs->rabqsk", both, np.eye(4)).reshape(256, 128)
    shift = (quad % 2) / 2.0
    angle = turn * m1[:, :, None, None] * (p[None, :] + shift[:, None]) / NPHI
    twiddle = np.stack([np.cos(angle), np.sin(angle)]).reshape(2, 128, 128)
    angle = turn * (p[:, None] * m2[None, :] % 128) / 128
    c, s = np.cos(angle) * keep, np.sin(angle) * keep
    square = np.array([[c, -s], [s, c]])
    second = np.einsum("iopm,ab->aipobm", square, np.eye(2)).reshape(512, 256)
    angle = np.tile(np.pi * m2 / 128, 2)
    half = np.stack([np.cos(angle), np.sin(angle)])
    half = np.concatenate([half, np.zeros((6, 128))])
    back = []
    for odd in range(2):
        angle = turn * m2[:, None] * (p[None, :] + odd / 2.0) / 128
        value = np.stack([np.cos(angle), np.sin(angle)]) * keep[None, :, None]
        back.append(np.einsum("rmp,ab->ambrp", value, np.eye(2)).reshape(128, 512))
    back = np.stack(back)
    odd = np.arange(2) / 2.0
    angle = turn * m1[None, :, :, None] * (p + odd[:, None, None, None]) / NPHI
    unwind = np.stack([np.cos(angle), np.sin(angle)], axis=1).reshape(2, 2, 2, 16, 1, 128)
    angle = turn * (m1[:, :, None] * kb % 32) / 32
    both = np.stack([np.cos(angle), -np.sin(angle)], axis=1)
    last = np.einsum("aihk,uv->ukaihv", both, np.eye(8)).reshape(256, 512)
    back_parts = halves(back)
    return (
        *halves(first),
        twiddle.astype(np.float32),
        *halves(second),
        half.astype(np.float32),
        np.concatenate(back_parts, axis=1),
        unwind.astype(np.float32),
        *halves(last),
    )


def place(index):
    return (index // LOCAL, lax.rem(index, LOCAL))


def kernel(*refs):
    (
        w_ref, off_ref, ids_ref, mt_ref, leg_ref,
        first_h, first_l, twiddle, second_h, second_l, half, back, unwind, last_h, last_l,
        kappa_ref, potential_ref,
        leg, out1, in1, out2, in2, out3, in3, id1, id2, sel, pick, filt, syn,
        barrier_dummy, leg_sem, send_sem, recv_sem,
    ) = refs
    del barrier_dummy
    band = lax.axis_index("blk")
    local = lax.axis_index("ma")
    me = band * LOCAL + local

    for j in range(SLOTS):
        pltpu.make_async_copy(leg_ref.at[j], leg.at[j], leg_sem.at[j]).start()

    barrier = pltpu.get_barrier_semaphore()

    def greet(i, carry):
        pl.semaphore_signal(
            barrier, inc=1, device_id=place(lax.rem(me + i, DEVICES)), device_id_type=MESH_IDS
        )
        return carry

    lax.fori_loop(1, DEVICES, greet, 0)

    def send(src, dst, k, target):
        pltpu.make_async_remote_copy(
            src_ref=src,
            dst_ref=dst,
            send_sem=send_sem.at[k],
            recv_sem=recv_sem.at[k],
            device_id=target,
            device_id_type=MESH_IDS,
        ).start()

    def settle(ref, k):
        pltpu.make_async_copy(ref, ref, recv_sem.at[k]).wait()

    def sent(ref, k):
        pltpu.make_async_copy(ref, ref, send_sem.at[k]).wait()

    def exchange(out, into, k):
        pltpu.make_async_copy(out.at[me], into.at[me], recv_sem.at[k]).start()

        def one(i, carry):
            t = lax.rem(me + i, DEVICES)
            send(out.at[t], into.at[me], k, place(t))
            return carry

        lax.fori_loop(1, DEVICES, one, 0)

    pl.semaphore_wait(barrier, DEVICES - 1)

    pltpu.make_async_copy(ids_ref.at[local], id1.at[local], recv_sem.at[3]).start()
    for i in range(1, LOCAL):
        t = lax.rem(local + i, LOCAL)
        send(ids_ref.at[t], id1.at[local], 3, (band, t))

    pixel = iota((128, 128), 0)
    group_of_row = iota((32, 128), 0) // 4

    def deposit(i, carry):
        t = lax.rem(me + i, DEVICES)
        w = w_ref[t]
        offs = off_ref[t]
        left = jnp.concatenate(
            [jnp.where(group_of_row == c, w, jnp.zeros_like(w)) for c in range(CAP)], axis=1
        )
        right = jnp.concatenate(
            [as_one_hot(offs[c : c + 1, :] == pixel) for c in range(CAP)], axis=1
        )
        out1[t] = nt(left, right).astype(bf16)
        return t

    t = deposit(0, 0)
    pltpu.make_async_copy(out1.at[t], in1.at[me], recv_sem.at[0]).start()

    def deposit_send(i, carry):
        t = deposit(i, carry)
        send(out1.at[t], in1.at[me], 0, place(t))
        return carry

    lax.fori_loop(1, 64, deposit_send, 0)

    settle(id1, 3)
    pltpu.make_async_copy(id1, id2.at[band], recv_sem.at[4]).start()
    for i in range(1, BANDS):
        t = lax.rem(band + i, BANDS)
        send(id1, id2.at[band], 4, (t, local))

    lax.fori_loop(64, DEVICES, deposit_send, 0)

    lane = iota((1, 2048), 1)
    m2 = lane % 64
    label = jnp.where(m2 < 48, lane // 128 * 2 + lane // 64 % 2 + 32 * m2, -1)
    for j in range(SLOTS):
        pick[pl.ds(128 * j, 128), :] = as_one_hot(mt_ref[:, j : j + 1] == label)

    settle(id2, 4)
    mine = as_one_hot(iota((8, 128), 1) == band * CAP + iota((8, 128), 0))
    ids_cs = nt(mine, id2[...].reshape(DEVICES, 128).astype(bf16)).astype(bf16)
    wide = as_one_hot(iota((128, 4096), 0) == iota((128, 4096), 1) // 32)
    spread = nn(ids_cs, wide)
    lane = iota((8, 4096), 1)
    spread = jnp.where(lane // 4 % 8 == iota((8, 4096), 0), spread, 0.0)
    ids_row = jnp.sum(spread, axis=0, keepdims=True)
    bin_row = (iota((1, 4096), 1) % 4).astype(f32)
    ids_row = jnp.where(ids_row < 0.0, -1.0, ids_row + 128.0 * bin_row)
    for b in range(NBIN):
        rows = (iota((128, 4096), 0) + 128 * b).astype(f32)
        sel[pl.ds(128 * b, 128), :] = as_one_hot(ids_row == rows)

    settle(in1, 0)
    counted = nn(sel[...], in1[...].reshape(4096, 128))

    lefts = []
    for b in range(NBIN):
        high, low = two_parts(counted[128 * b : 128 * b + 128])
        z = nn(first_h[...], high) + nn(first_h[...], low) + nn(first_l[...], high)
        zr, zi = z[:128], z[128:]
        ar = zr * twiddle[0] + zi * twiddle[1]
        ai = zi * twiddle[0] - zr * twiddle[1]
        lefts.append(jnp.concatenate([ar[:64], ai[:64], ar[64:], ai[64:]], axis=1))
    high, low = two_parts(jnp.concatenate(lefts, axis=0))
    x = nn(high, second_h[...]) + nn(low, second_h[...]) + nn(high, second_l[...])
    xr, xi = x[:, :128], x[:, 128:]
    odd = iota((256, 128), 0) % 2 == 1
    c = jnp.where(odd, half[0:1, :], 1.0)
    s = jnp.where(odd, half[1:2, :], 0.0)
    modes = jnp.concatenate([xr * c + xi * s, xi * c - xr * s], axis=0).astype(bf16)
    row, col = iota((512, 512), 0), iota((512, 512), 1)
    origin = row // 4 % 2 * 256 + row % 4 * 64 + row // 32 * 4 + row // 8 % 4
    modes = nn(as_one_hot(col == origin), modes).astype(bf16)
    modes = jnp.concatenate([modes[32 * h : 32 * h + 32] for h in range(16)], axis=1)
    chosen = [nt(modes, pick[pl.ds(128 * j, 128), :]) for j in range(SLOTS)]
    flat2 = out2.reshape(DEVICES * 4, 128)
    for q in range(4):
        block = jnp.concatenate(
            [y[8 * q : 8 * q + 8] for y in chosen] + [jnp.zeros((32, 128), f32)], axis=0
        )
        flat2[pl.ds(q, DEVICES, stride=4), :] = block.T
    exchange(out2, in2, 1)

    for j in range(SLOTS):
        pltpu.make_async_copy(leg_ref.at[j], leg.at[j], leg_sem.at[j]).wait()
    degree = iota((16, DEGREES), 1).astype(f32)
    gain = jnp.where(degree > 0.5, -20000.0 / jnp.maximum(degree * (degree + 1.0), 1.0), 0.0)
    gain = jnp.where(iota((16, DEGREES), 0) // 4 % 2 == 1, gain, 1.0)
    row = iota((192, 128), 0)
    doubled = as_one_hot(iota((192, 128), 1) == row // 16 * 8 + row // 8 % 2 * 4 + row % 4)

    settle(in2, 1)
    mode_rows = nt(doubled, in2[...].reshape(CYCLES, 128).astype(bf16)).astype(bf16)
    for j in range(SLOTS):
        filt[j] = (nt(mode_rows[16 * j : 16 * j + 16], leg[j]) * gain).astype(bf16)
    for j in range(SLOTS):
        syn[pl.ds(16 * j, 16), :] = nn(filt[j], leg[j]).astype(bf16)

    col = iota((512, 512), 1)
    by_quad = as_one_hot(iota((512, 512), 0) == col % 128 * 4 + col // 128)
    maps = nn(syn[...], by_quad)
    flat3 = out3.reshape(DEVICES * 8, 128)
    for h in range(6):
        block = jnp.concatenate(
            [
                maps[16 * j : 16 * j + 16, 128 * q : 128 * q + 128]
                for j in (2 * h, 2 * h + 1)
                for q in range(4)
            ],
            axis=0,
        )
        flat3[pl.ds(h, DEVICES, stride=8), :] = block.T
    for h in range(6, 8):
        flat3[pl.ds(h, DEVICES, stride=8), :] = jnp.zeros((DEVICES, 128), f32)
    exchange(out3, in3, 2)
    settle(in3, 2)

    flat3 = in3.reshape(DEVICES * 8, 128)
    lefts = []
    for h in range(6):
        block = flat3[pl.ds(h, DEVICES, stride=8), :].T.astype(bf16)
        lefts += [block[:64], block[64:]]
    v = nn(jnp.concatenate(lefts, axis=1), pick[...])
    v = (v * jnp.where(iota((1, 2048), 1) == 0, 1.0, 2.0)).astype(bf16)
    rights = [None] * 4
    for odd in range(2):
        left = jnp.concatenate(
            [
                v[16 * q : 16 * q + 16, 128 * h : 128 * h + 128]
                for h in range(16)
                for q in (odd, odd + 2)
            ],
            axis=0,
        )
        g = nn(jnp.concatenate([left, left], axis=1), back[odd])
        g = g.reshape(16, 2, 2, 8, 512)
        parts = ([], [])
        for par in range(2):
            at = 256 * par
            g0c, g0s = g[:, :, 0, :, at : at + 128], g[:, :, 0, :, at + 128 : at + 256]
            g1c, g1s = g[:, :, 1, :, at : at + 128], g[:, :, 1, :, at + 128 : at + 256]
            ur, ui = g0c - g1s, g0s + g1c
            tc, ts = unwind[odd, 0, par][:, None], unwind[odd, 1, par][:, None]
            er, ei = ur * tc - ui * ts, ur * ts + ui * tc
            for k in range(2):
                parts[k].append(er[:, k].reshape(128, 128))
                parts[k].append(ei[:, k].reshape(128, 128))
        for k in range(2):
            rights[odd + 2 * k] = jnp.concatenate(parts[k], axis=0)
    for k in range(2):
        high, low = two_parts(jnp.concatenate(rights[2 * k : 2 * k + 2], axis=1))
        sky = nn(last_h[...], high) + nn(last_h[...], low) + nn(last_l[...], high)
        for q in range(2):
            one = sky[:, 128 * q : 128 * q + 128].reshape(2, 4, 32, 128)
            kappa_ref[:, 2 * k + q] = one[0]
            potential_ref[:, 2 * k + q] = one[1]

    sent(id1.at[pl.ds(0, LOCAL - 1)], 3)
    sent(id2.at[pl.ds(0, BANDS - 1)], 4)
    sent(in1.at[pl.ds(0, DEVICES - 1)], 0)
    sent(in2.at[pl.ds(0, DEVICES - 1)], 1)
    sent(in3.at[pl.ds(0, DEVICES - 1)], 2)


def per_device(weights, offsets, counts, block_ids, m_table, legendre):
    live = lax.broadcasted_iota(jnp.int32, (DEVICES, CAP), 1) < counts[0][:, None]
    ids = jnp.where(live, block_ids[0], -1).astype(f32)
    ids = ids.reshape(BANDS, LOCAL, CAP).transpose(1, 0, 2).reshape(LOCAL, 1, BANDS * CAP)
    constants = [jnp.asarray(t) for t in tables()]
    vmem = pl.BlockSpec(memory_space=pltpu.VMEM)
    hbm = pl.BlockSpec(memory_space=pltpu.HBM)
    shape = jax.ShapeDtypeStruct((NBIN, 4, 32, 128), f32)
    kappa, potential = pl.pallas_call(
        kernel,
        out_shape=(shape, shape),
        in_specs=[vmem] * 4 + [hbm] + [vmem] * len(constants),
        out_specs=(vmem, vmem),
        scratch_shapes=[
            pltpu.VMEM((SLOTS, DEGREES, CYCLES), bf16),
            pltpu.VMEM((DEVICES, 32, 128), bf16),
            pltpu.VMEM((DEVICES, 32, 128), bf16),
            pltpu.VMEM((DEVICES, 4, 128), f32),
            pltpu.VMEM((DEVICES, 4, 128), f32),
            pltpu.VMEM((DEVICES, 8, 128), f32),
            pltpu.VMEM((DEVICES, 8, 128), f32),
            pltpu.VMEM((LOCAL, 1, 128), f32),
            pltpu.VMEM((BANDS, LOCAL, 1, 128), f32),
            pltpu.VMEM((512, 4096), bf16),
            pltpu.VMEM((SLOTS * 128, 2048), bf16),
            pltpu.VMEM((SLOTS, 16, DEGREES), bf16),
            pltpu.VMEM((SLOTS * 16, CYCLES), bf16),
            pltpu.VMEM((8, 128), f32),
            pltpu.SemaphoreType.DMA((SLOTS,)),
            pltpu.SemaphoreType.DMA((5,)),
            pltpu.SemaphoreType.DMA((5,)),
        ],
        compiler_params=pltpu.CompilerParams(
            collective_id=0, has_side_effects=True, vmem_limit_bytes=60 << 20
        ),
        name="deposit_filter",
    )(
        weights[0].reshape(DEVICES, CAP * NBIN, 128),
        offsets[0],
        ids,
        m_table.reshape(DEVICES, SLOTS),
        legendre,
        *constants,
    )
    return kappa.reshape(NBIN, 4, NPHI), potential.reshape(NBIN, 4, NPHI)


def solution(mesh):
    placed = (
        P(("blk", "ma"), None, None, None, None),
        P(("blk", "ma"), None, None, None),
        P(("blk", "ma"), None),
        P(("blk", "ma"), None, None),
        P(),
        P(("blk", "ma"), None, None),
    )
    return jax.shard_map(
        per_device,
        mesh=mesh,
        in_specs=placed,
        out_specs=(P(None, ("blk", "ma"), None), P(None, ("blk", "ma"), None)),
        check_vma=False,
    )
```

time: 239 us -> 87.8 us (0.37); the launches traced: 235 us -> 87.5 us
  Pallas kernels: 0 us -> 78.5 us
  local copies, waits for them, and re-layouts: 81.3 us -> 7.07 us
  matrix products: 70.6 us -> 0 us
  waiting for transfers between devices: 45 us -> 0 us
  starting transfers between devices: 30.6 us -> 0 us
  other arithmetic: 6.02 us -> 1.33 us
    pallas_call x0 -> x1, Pallas kernels: none -> 78.5 us  [per_device(): pl.pallas_call(kernel, out_shape=(shape, shape), in_specs=[vmem] * 4 + [h...]
    dot_general x16 -> x0, matrix products: 70.6 us -> none  [the longest x1 30.7 us: per_device(): jnp.einsum('dcbs,dcsp->dcbp', groups, onehot, preferred_element_type=jnp....]
    all_to_all x4 -> x0, waiting for transfers between devices: 45 us -> none  [the longest x1 24.7 us: per_device(): lax.all_to_all(partial_value, ('blk', 'ma'), split_axis=0, concat_axis=0,...]
    all_to_all x4 -> x0, starting transfers between devices: 30.6 us -> none  [the longest x1 11.5 us: per_device(): lax.all_to_all(sent_ids, ('blk', 'ma'), split_axis=0, concat_axis=0, tile...]
    gather x4 -> x0, local copies, waits for them, and re-layouts: 19.4 us -> none  [the longest x2 13.7 us: per_device(): imag_part = jnp.take(spectrum_imag, m_table, axis=1)]
    unnamed x23 -> x1, local copies, waits for them, and re-layouts: 16.7 us -> 0.51 us
    scatter x2 -> x0, local copies, waits for them, and re-layouts: 11 us -> none  [per_device(): jnp.zeros((row_total, cycle_length), jnp.float32).at[:, m_table]]
    convert_element_type x3 -> x0, local copies, waits for them, and re-layouts: 10.9 us -> none  [the longest x2 9.78 us: per_device(): values = lax.all_to_all(outgoing_maps, ('blk', 'ma'), split_axis=4, conca...]
  transfers between devices with their start and end apart: 4 -> 0, of which waited for: 3 -> 0; matrix products, arithmetic and copies ran while one was open for 16% -> 0% of each run, Pallas kernels for 0% -> 0%
where the time goes in v1:
time: 87.8 us; the launch traced here: 87.5 us
  Pallas kernels  78.5 us (89%)
  local copies, waits for them, and re-layouts  7.07 us (8%)
  other arithmetic  1.33 us (2%)
    pallas_call x1, Pallas kernels, per_device(): pl.pallas_call(kernel, out_shape=(shape, shape), in_specs=[vmem] * 4 + [h...  78.5 us
    reshape x2, local copies, waits for them, and re-layouts, per_device(): return (kappa.reshape(NBIN, 4, NPHI), potential.reshape(NBIN, 4, NPHI))  3.48 us

profile of v1, /device:TPU:1, one launch (start us, length us, event | category | flops | bytes accessed | tf_op | source)
XLA Modules:
  0.0 87.5 jit_solution(2709065236080416258)
XLA Ops:
  0.6 0.5 broadcast.6
  1.1 1.3 %reduce.3 = s32[128]{0:T(128)S(1)} reduce(s32[1,128]{1,0:T(1,128)} %param.18, s32[]{:T(128)} %broadcast.6), dimensions={0}, to_apply=%param.18.reduce_sub_computation.3 | reduce | bytes 1028 | tf_op args[2]
  2.5 0.1 lt.11
  2.5 0.8 squeeze.7
  3.3 0.1 copy.20
  3.4 0.7 reshape.25
  4.1 1.4 %reshape.26.refs_3_ = s32[128,12]{1,0:T(8,128)} reshape(s32[1536]{0:T(1024)} %param.20) | data formatting | bytes 12288 | tf_op jit(solution)/shard_map/reshape | solution.py:365
  5.6 78.5 %deposit_filter.1 = (f32[4,4,32,128]{3,2,1,0:T(8,128)}, f32[4,4,32,128]{3,2,1,0:T(8,128)}) custom-call(bf16[128,32,128]{2,1,0:T(8,128)(2,1)} %bitcast.11, s32[128,8,128]{2,1,0:T(8,128)} %bitcast.12, f32[8,1,128]{2,1,0:T(1,128)} %bitcast.13, s32[128,12]{1,0:T(8,128)} %reshape.26.refs_3_, bf16[12,1664,512]{2,1,0:T(8,128)(2,1)} %refs_4_.1, ...), custom_call_target="tpu_custom_call" | custom-call | tf_op jit(solution)/shard_map/deposit_filter/pallas_call | solution.py:333
  84.0 1.7 %reshape.27 = f32[4,4,4096]{2,1,0:T(4,128)} reshape(f32[4,4,32,128]{3,2,1,0:T(8,128)} %get-tuple-element.4) | data formatting | bytes 524288 | tf_op jit(solution)/shard_map/reshape | solution.py:369
  85.8 1.7 %reshape.28 = f32[4,4,4096]{2,1,0:T(4,128)} reshape(f32[4,4,32,128]{3,2,1,0:T(8,128)} %get-tuple-element.5) | data formatting | bytes 524288 | tf_op jit(solution)/shard_map/reshape | solution.py:369
  (1 shorter events, 0.0 us)

commit v2 on v1

--- a/solution.py
+++ b/solution.py
@@ -17,6 +17,9 @@
 SLOTS = 12
 DEGREES = 1664
 CYCLES = 512
+PART = 32
+BATCH = 8
+EARLY = 16
 MESH_IDS = pl.DeviceIdType.MESH
 bf16 = jnp.bfloat16
 f32 = jnp.float32
@@ -99,19 +102,18 @@
 
 def kernel(*refs):
     (
-        w_ref, off_ref, ids_ref, mt_ref, leg_ref,
-        first_h, first_l, twiddle, second_h, second_l, half, back, unwind, last_h, last_l,
-        kappa_ref, potential_ref,
-        leg, out1, in1, out2, in2, out3, in3, id1, id2, sel, pick, filt, syn,
-        barrier_dummy, leg_sem, send_sem, recv_sem,
-    ) = refs
-    del barrier_dummy
+        w_ref, off_ref, blocks_ref, counts_ref, orders_ref, leg_ref, *constants,
+    ) = refs[:16]
+    kappa_ref, potential_ref = refs[16:18]
+    held = refs[18:28]
+    first_h, first_l, twiddle, second_h, second_l, half, back, unwind, last_h, last_l = held
+    (
+        leg, out1, in1, out2, in2, out3, in3, id0, id1, idx, id2, sel, pick, filt, syn,
+        const_sem, leg_sem, send_sem, recv_sem, part_sem,
+    ) = refs[28:]
     band = lax.axis_index("blk")
     local = lax.axis_index("ma")
     me = band * LOCAL + local
-
-    for j in range(SLOTS):
-        pltpu.make_async_copy(leg_ref.at[j], leg.at[j], leg_sem.at[j]).start()
 
     barrier = pltpu.get_barrier_semaphore()
 
@@ -149,69 +151,120 @@
 
         lax.fori_loop(1, DEVICES, one, 0)
 
-    pl.semaphore_wait(barrier, DEVICES - 1)
-
-    pltpu.make_async_copy(ids_ref.at[local], id1.at[local], recv_sem.at[3]).start()
-    for i in range(1, LOCAL):
-        t = lax.rem(local + i, LOCAL)
-        send(ids_ref.at[t], id1.at[local], 3, (band, t))
-
-    pixel = iota((128, 128), 0)
+    for n in range(10):
+        pltpu.make_async_copy(constants[n], held[n], const_sem.at[n]).start()
+    for j in range(SLOTS):
+        pltpu.make_async_copy(leg_ref.at[j], leg.at[j], leg_sem.at[j]).start()
+
+    pixel = iota((128, 128), 0).astype(f32).astype(bf16)
     group_of_row = iota((32, 128), 0) // 4
 
     def deposit(i, carry):
         t = lax.rem(me + i, DEVICES)
         w = w_ref[t]
-        offs = off_ref[t]
+        offs = off_ref[t].astype(f32).astype(bf16)
         left = jnp.concatenate(
             [jnp.where(group_of_row == c, w, jnp.zeros_like(w)) for c in range(CAP)], axis=1
         )
+        one, zero = jnp.ones((), bf16), jnp.zeros((), bf16)
         right = jnp.concatenate(
-            [as_one_hot(offs[c : c + 1, :] == pixel) for c in range(CAP)], axis=1
-        )
-        out1[t] = nt(left, right).astype(bf16)
-        return t
-
-    t = deposit(0, 0)
-    pltpu.make_async_copy(out1.at[t], in1.at[me], recv_sem.at[0]).start()
-
-    def deposit_send(i, carry):
-        t = deposit(i, carry)
-        send(out1.at[t], in1.at[me], 0, place(t))
+            [jnp.where(offs[c : c + 1, :] == pixel, one, zero) for c in range(CAP)], axis=1
+        )
+        out1[i] = nt(left, right).astype(bf16)
         return carry
 
-    lax.fori_loop(1, 64, deposit_send, 0)
+    def send_part(i, k):
+        pltpu.make_async_remote_copy(
+            src_ref=out1.at[i],
+            dst_ref=in1.at[i],
+            send_sem=send_sem.at[0],
+            recv_sem=part_sem.at[k],
+            device_id=place(lax.rem(me + i, DEVICES)),
+            device_id_type=MESH_IDS,
+        ).start()
+
+    live = iota((CAP, DEVICES), 0) < counts_ref[...]
+    id0[...] = jnp.where(live, blocks_ref[...], -1).astype(f32)
+    lax.fori_loop(0, EARLY, deposit, 0, unroll=4)
+    pl.semaphore_wait(barrier, DEVICES - 1)
+
+    pltpu.make_async_copy(id0, id1.at[local], recv_sem.at[3]).start()
+    for i in range(1, LOCAL):
+        send(id0, id1.at[local], 3, (band, lax.rem(local + i, LOCAL)))
+
+    pltpu.make_async_copy(out1.at[0], in1.at[0], part_sem.at[0]).start()
+
+    def early(i, carry):
+        send_part(i, 0)
+        return carry
+
+    lax.fori_loop(1, EARLY, early, 0)
+
+    def deposit_send(k):
+        def step(n, carry):
+            for u in range(BATCH):
+                deposit(n * BATCH + u, carry)
+            for u in range(BATCH):
+                send_part(n * BATCH + u, k)
+            return carry
+
+        return step
+
+    lax.fori_loop(EARLY // BATCH, PART // BATCH, deposit_send(0), 0)
+    lax.fori_loop(1 * PART // BATCH, 2 * PART // BATCH, deposit_send(1), 0)
 
     settle(id1, 3)
-    pltpu.make_async_copy(id1, id2.at[band], recv_sem.at[4]).start()
+    column = as_one_hot(iota((BANDS, DEVICES), 1) == iota((BANDS, DEVICES), 0) * LOCAL + local)
+    every = id1[...].reshape(LOCAL * CAP, DEVICES).astype(bf16)
+    every = nt(column, jnp.concatenate([every, every], axis=0))
+    for i in range(BANDS):
+        idx[i] = every[i : i + 1]
+    pltpu.make_async_copy(idx.at[band], id2.at[band], recv_sem.at[4]).start()
     for i in range(1, BANDS):
         t = lax.rem(band + i, BANDS)
-        send(id1, id2.at[band], 4, (t, local))
-
-    lax.fori_loop(64, DEVICES, deposit_send, 0)
+        send(idx.at[t], id2.at[band], 4, (t, local))
+
+    lax.fori_loop(2 * PART // BATCH, 3 * PART // BATCH, deposit_send(2), 0)
+    lax.fori_loop(3 * PART // BATCH, 4 * PART // BATCH, deposit_send(3), 0)
+
+    slot = iota((DEVICES, 1536), 1)
+    owner = (slot * 5462) >> 16
+    orders = jnp.broadcast_to(orders_ref[...].reshape(1, 1536), (DEVICES, 1536)).astype(f32)
+    orders = jnp.where(owner == iota((DEVICES, 1536), 0), orders, 0.0)
+    slot = iota((16, 1536), 1)
+    which = as_one_hot(slot - ((slot * 5462) >> 16) * SLOTS == iota((16, 1536), 0))
+    high, low = two_parts(orders)
+    orders = nt(high, which) + nt(low, which)
 
     lane = iota((1, 2048), 1)
     m2 = lane % 64
-    label = jnp.where(m2 < 48, lane // 128 * 2 + lane // 64 % 2 + 32 * m2, -1)
+    label = jnp.where(m2 < 48, lane // 128 * 2 + lane // 64 % 2 + 32 * m2, -1).astype(f32)
     for j in range(SLOTS):
-        pick[pl.ds(128 * j, 128), :] = as_one_hot(mt_ref[:, j : j + 1] == label)
+        pick[pl.ds(128 * j, 128), :] = as_one_hot(orders[:, j : j + 1] == label)
 
     settle(id2, 4)
-    mine = as_one_hot(iota((8, 128), 1) == band * CAP + iota((8, 128), 0))
-    ids_cs = nt(mine, id2[...].reshape(DEVICES, 128).astype(bf16)).astype(bf16)
-    wide = as_one_hot(iota((128, 4096), 0) == iota((128, 4096), 1) // 32)
-    spread = nn(ids_cs, wide)
-    lane = iota((8, 4096), 1)
-    spread = jnp.where(lane // 4 % 8 == iota((8, 4096), 0), spread, 0.0)
+    at = iota((128, 4096), 1)
+    source = me + DEVICES - (at >> 5)
+    wide = as_one_hot(iota((128, 4096), 0) == (source & 7) * CAP + ((at >> 2) & 7))
+    spread = nn(id2[...].reshape(BANDS, 128).astype(bf16), wide)
+    at = iota((BANDS, 4096), 1)
+    source = me + DEVICES - (at >> 5)
+    spread = jnp.where(((source >> 3) & 15) == iota((BANDS, 4096), 0), spread, 0.0)
     ids_row = jnp.sum(spread, axis=0, keepdims=True)
-    bin_row = (iota((1, 4096), 1) % 4).astype(f32)
+    bin_row = (iota((1, 4096), 1) & 3).astype(f32)
     ids_row = jnp.where(ids_row < 0.0, -1.0, ids_row + 128.0 * bin_row)
     for b in range(NBIN):
         rows = (iota((128, 4096), 0) + 128 * b).astype(f32)
         sel[pl.ds(128 * b, 128), :] = as_one_hot(ids_row == rows)
 
-    settle(in1, 0)
-    counted = nn(sel[...], in1[...].reshape(4096, 128))
+    for n in range(10):
+        pltpu.make_async_copy(constants[n], held[n], const_sem.at[n]).wait()
+    counted = None
+    for k in range(4):
+        piece = in1.at[pl.ds(PART * k, PART)]
+        pltpu.make_async_copy(piece, piece, part_sem.at[k]).wait()
+        term = nn(sel[:, 1024 * k : 1024 * k + 1024], piece[...].reshape(1024, 128))
+        counted = term if counted is None else counted + term
 
     lefts = []
     for b in range(NBIN):
@@ -312,8 +365,9 @@
         sky = nn(last_h[...], high) + nn(last_h[...], low) + nn(last_l[...], high)
         for q in range(2):
             one = sky[:, 128 * q : 128 * q + 128].reshape(2, 4, 32, 128)
-            kappa_ref[:, 2 * k + q] = one[0]
-            potential_ref[:, 2 * k + q] = one[1]
+            for b in range(NBIN):
+                kappa_ref[b, pl.ds(2 * k + q, 32, stride=4), :] = one[0, b]
+                potential_ref[b, pl.ds(2 * k + q, 32, stride=4), :] = one[1, b]
 
     sent(id1.at[pl.ds(0, LOCAL - 1)], 3)
     sent(id2.at[pl.ds(0, BANDS - 1)], 4)
@@ -322,20 +376,29 @@
     sent(in3.at[pl.ds(0, DEVICES - 1)], 2)
 
 
+def hand_over(kappa, potential, kappa_out, potential_out, sems):
+    copies = [
+        pltpu.make_async_copy(kappa, kappa_out, sems.at[0]),
+        pltpu.make_async_copy(potential, potential_out, sems.at[1]),
+    ]
+    for copy in copies:
+        copy.start()
+    for copy in copies:
+        copy.wait()
+
+
 def per_device(weights, offsets, counts, block_ids, m_table, legendre):
-    live = lax.broadcasted_iota(jnp.int32, (DEVICES, CAP), 1) < counts[0][:, None]
-    ids = jnp.where(live, block_ids[0], -1).astype(f32)
-    ids = ids.reshape(BANDS, LOCAL, CAP).transpose(1, 0, 2).reshape(LOCAL, 1, BANDS * CAP)
     constants = [jnp.asarray(t) for t in tables()]
     vmem = pl.BlockSpec(memory_space=pltpu.VMEM)
     hbm = pl.BlockSpec(memory_space=pltpu.HBM)
-    shape = jax.ShapeDtypeStruct((NBIN, 4, 32, 128), f32)
+    shape = jax.ShapeDtypeStruct((NBIN, 128, 128), f32)
     kappa, potential = pl.pallas_call(
         kernel,
         out_shape=(shape, shape),
-        in_specs=[vmem] * 4 + [hbm] + [vmem] * len(constants),
+        in_specs=[vmem] * 5 + [hbm] * 11,
         out_specs=(vmem, vmem),
         scratch_shapes=[
+            *[pltpu.VMEM(t.shape, t.dtype) for t in constants],
             pltpu.VMEM((SLOTS, DEGREES, CYCLES), bf16),
             pltpu.VMEM((DEVICES, 32, 128), bf16),
             pltpu.VMEM((DEVICES, 32, 128), bf16),
@@ -343,16 +406,19 @@
             pltpu.VMEM((DEVICES, 4, 128), f32),
             pltpu.VMEM((DEVICES, 8, 128), f32),
             pltpu.VMEM((DEVICES, 8, 128), f32),
-            pltpu.VMEM((LOCAL, 1, 128), f32),
-            pltpu.VMEM((BANDS, LOCAL, 1, 128), f32),
+            pltpu.VMEM((CAP, DEVICES), f32),
+            pltpu.VMEM((LOCAL, CAP, DEVICES), f32),
+            pltpu.VMEM((BANDS, 1, 128), f32),
+            pltpu.VMEM((BANDS, 1, 128), f32),
             pltpu.VMEM((512, 4096), bf16),
             pltpu.VMEM((SLOTS * 128, 2048), bf16),
             pltpu.VMEM((SLOTS, 16, DEGREES), bf16),
             pltpu.VMEM((SLOTS * 16, CYCLES), bf16),
-            pltpu.VMEM((8, 128), f32),
+            pltpu.SemaphoreType.DMA((10,)),
             pltpu.SemaphoreType.DMA((SLOTS,)),
             pltpu.SemaphoreType.DMA((5,)),
             pltpu.SemaphoreType.DMA((5,)),
+            pltpu.SemaphoreType.DMA((4,)),
         ],
         compiler_params=pltpu.CompilerParams(
             collective_id=0, has_side_effects=True, vmem_limit_bytes=60 << 20
@@ -361,12 +427,22 @@
     )(
         weights[0].reshape(DEVICES, CAP * NBIN, 128),
         offsets[0],
-        ids,
-        m_table.reshape(DEVICES, SLOTS),
+        jnp.swapaxes(block_ids, 1, 2).reshape(CAP, DEVICES),
+        counts,
+        m_table,
         legendre,
         *constants,
     )
-    return kappa.reshape(NBIN, 4, NPHI), potential.reshape(NBIN, 4, NPHI)
+    kappa, potential = pl.pallas_call(
+        hand_over,
+        out_shape=(shape, shape),
+        in_specs=[vmem, vmem],
+        out_specs=(hbm, hbm),
+        scratch_shapes=[pltpu.SemaphoreType.DMA((2,))],
+        name="hand_over",
+    )(kappa, potential)
+    maps = [x.reshape(NBIN, 32, 4, 128).transpose(0, 2, 1, 3) for x in (kappa, potential)]
+    return tuple(x.reshape(NBIN, 4, NPHI) for x in maps)
 
 
 def solution(mesh):

time: 87.8 us -> 70.5 us (0.80)
  Pallas kernels: 78.5 us -> 69.5 us
  local copies, waits for them, and re-layouts: 7.07 us -> 0 us
  other arithmetic: 1.33 us -> 0 us
    pallas_call x1 -> x2, Pallas kernels: 78.5 us -> 69.5 us  [the longest x1 67.7 us: per_device(): pl.pallas_call(kernel, out_shape=(shape, shape), in_specs=[vmem] * 5 + [h...]
    reshape x4 -> x0, local copies, waits for them, and re-layouts: 5.59 us -> none  [the longest x2 3.48 us: per_device(): return (kappa.reshape(NBIN, 4, NPHI), potential.reshape(NBIN, 4, NPHI))]
    unnamed x1 -> x0, other arithmetic: 1.32 us -> none
where the time goes in v2:
time: 70.5 us; the launch traced here: 70.3 us
  Pallas kernels  69.5 us (99%)
  between operations  0.8 us (1%)
    pallas_call x1, Pallas kernels, per_device(): pl.pallas_call(kernel, out_shape=(shape, shape), in_specs=[vmem] * 5 + [h...  67.7 us
    pallas_call x1, Pallas kernels, per_device(): pl.pallas_call(hand_over, out_shape=(shape, shape), in_specs=[vmem, vmem]...  1.83 us

profile of v2, /device:TPU:1, one launch (start us, length us, event | category | flops | bytes accessed | tf_op | source)
XLA Modules:
  0.0 70.3 jit_solution(3209911255219239039)
XLA Ops:
  0.6 67.7 %deposit_filter.1 = (f32[4,128,128]{2,1,0:T(8,128)}, f32[4,128,128]{2,1,0:T(8,128)}) custom-call(bf16[128,32,128]{2,1,0:T(8,128)(2,1)} %bitcast.15, s32[128,8,128]{2,1,0:T(8,128)} %bitcast.16, s32[8,128]{1,0:T(8,128)} %bitcast.17, s32[1,128]{1,0:T(1,128)} %refs_3_.1, s32[1536]{0:T(1024)} %refs_4_.1, bf16[12,1664,512]{2,1,0:T(8,128)(2,1)} %refs_5_.1, ...), custom_call_target="tpu_custom_call" | custom-call | tf_op jit(solution)/shard_map/deposit_filter/pallas_call | solution.py:395
  68.3 1.8 %hand_over.1 = (f32[4,128,128]{2,1,0:T(8,128)}, f32[4,128,128]{2,1,0:T(8,128)}) custom-call(f32[4,128,128]{2,1,0:T(8,128)} %get-tuple-element.6.kappa, f32[4,128,128]{2,1,0:T(8,128)} %get-tuple-element.7.potential), custom_call_target="tpu_custom_call" | custom-call | tf_op jit(solution)/shard_map/hand_over/pallas_call | solution.py:436

commit v3 on v2

--- a/solution.py
+++ b/solution.py
@@ -12,6 +12,7 @@
 BANDS = 16
 LOCAL = 8
 DEVICES = BANDS * LOCAL
+CHIPS = DEVICES // 2
 CAP = 8
 NBIN = 4
 SLOTS = 12
@@ -19,6 +20,7 @@
 CYCLES = 512
 PART = 32
 BATCH = 8
+STRIDE = 27
 EARLY = 16
 MESH_IDS = pl.DeviceIdType.MESH
 bf16 = jnp.bfloat16
@@ -108,12 +110,15 @@
     held = refs[18:28]
     first_h, first_l, twiddle, second_h, second_l, half, back, unwind, last_h, last_l = held
     (
-        leg, out1, in1, out2, in2, out3, in3, id0, id1, idx, id2, sel, pick, filt, syn,
+        leg, out1, in1, near2, out2, in2, near3, got3, out3, in3, stage, id0, id1, idx, id2, sel, pick, filt, syn,
         const_sem, leg_sem, send_sem, recv_sem, part_sem,
     ) = refs[28:]
     band = lax.axis_index("blk")
     local = lax.axis_index("ma")
     me = band * LOCAL + local
+    core = lax.rem(local, 2)
+    chip = me // 2
+    sibling = (band, local + 1 - 2 * core)
 
     barrier = pltpu.get_barrier_semaphore()
 
@@ -142,14 +147,14 @@
         pltpu.make_async_copy(ref, ref, send_sem.at[k]).wait()
 
     def exchange(out, into, k):
-        pltpu.make_async_copy(out.at[me], into.at[me], recv_sem.at[k]).start()
+        pltpu.make_async_copy(out.at[chip], into.at[chip], recv_sem.at[k]).start()
 
         def one(i, carry):
-            t = lax.rem(me + i, DEVICES)
-            send(out.at[t], into.at[me], k, place(t))
+            t = lax.rem(chip + i, CHIPS)
+            send(out.at[t], into.at[chip], k, place(2 * t + core))
             return carry
 
-        lax.fori_loop(1, DEVICES, one, 0)
+        lax.fori_loop(1, CHIPS, one, 0)
 
     for n in range(10):
         pltpu.make_async_copy(constants[n], held[n], const_sem.at[n]).start()
@@ -159,8 +164,13 @@
     pixel = iota((128, 128), 0).astype(f32).astype(bf16)
     group_of_row = iota((32, 128), 0) // 4
 
+    def target(i):
+        step = lax.rem(i * STRIDE, DEVICES)
+        return lax.rem(band + step // LOCAL, BANDS), lax.rem(local + lax.rem(step, LOCAL), LOCAL)
+
     def deposit(i, carry):
-        t = lax.rem(me + i, DEVICES)
+        t = target(i)
+        t = t[0] * LOCAL + t[1]
         w = w_ref[t]
         offs = off_ref[t].astype(f32).astype(bf16)
         left = jnp.concatenate(
@@ -179,7 +189,7 @@
             dst_ref=in1.at[i],
             send_sem=send_sem.at[0],
             recv_sem=part_sem.at[k],
-            device_id=place(lax.rem(me + i, DEVICES)),
+            device_id=target(i),
             device_id_type=MESH_IDS,
         ).start()
 
@@ -230,11 +240,15 @@
     slot = iota((DEVICES, 1536), 1)
     owner = (slot * 5462) >> 16
     orders = jnp.broadcast_to(orders_ref[...].reshape(1, 1536), (DEVICES, 1536)).astype(f32)
-    orders = jnp.where(owner == iota((DEVICES, 1536), 0), orders, 0.0)
+    row = iota((DEVICES, 1536), 0)
+    device = 2 * (row & 63) + jnp.where(row < CHIPS, core, 1 - core)
+    orders = jnp.where(owner == device, orders, 0.0)
     slot = iota((16, 1536), 1)
     which = as_one_hot(slot - ((slot * 5462) >> 16) * SLOTS == iota((16, 1536), 0))
     high, low = two_parts(orders)
     orders = nt(high, which) + nt(low, which)
+
+    stage[...] = jnp.zeros_like(stage)
 
     lane = iota((1, 2048), 1)
     m2 = lane % 64
@@ -244,12 +258,12 @@
 
     settle(id2, 4)
     at = iota((128, 4096), 1)
-    source = me + DEVICES - (at >> 5)
-    wide = as_one_hot(iota((128, 4096), 0) == (source & 7) * CAP + ((at >> 2) & 7))
+    step = (at >> 5) * STRIDE & 127
+    wide = as_one_hot(iota((128, 4096), 0) == (local - step & 7) * CAP + ((at >> 2) & 7))
     spread = nn(id2[...].reshape(BANDS, 128).astype(bf16), wide)
     at = iota((BANDS, 4096), 1)
-    source = me + DEVICES - (at >> 5)
-    spread = jnp.where(((source >> 3) & 15) == iota((BANDS, 4096), 0), spread, 0.0)
+    step = (at >> 5) * STRIDE & 127
+    spread = jnp.where((band - (step >> 3) & 15) == iota((BANDS, 4096), 0), spread, 0.0)
     ids_row = jnp.sum(spread, axis=0, keepdims=True)
     bin_row = (iota((1, 4096), 1) & 3).astype(f32)
     ids_row = jnp.where(ids_row < 0.0, -1.0, ids_row + 128.0 * bin_row)
@@ -267,9 +281,13 @@
         counted = term if counted is None else counted + term
 
     lefts = []
+    high, low = two_parts(
+        jnp.concatenate([counted[128 * b : 128 * b + 128] for b in range(NBIN)], axis=1)
+    )
+    both = jnp.concatenate([first_h[...], first_l[...]], axis=1)
+    every = nn(both, jnp.concatenate([high, high], axis=0)) + nn(first_h[...], low)
     for b in range(NBIN):
-        high, low = two_parts(counted[128 * b : 128 * b + 128])
-        z = nn(first_h[...], high) + nn(first_h[...], low) + nn(first_l[...], high)
+        z = every[:, 128 * b : 128 * b + 128]
         zr, zi = z[:128], z[128:]
         ar = zr * twiddle[0] + zi * twiddle[1]
         ai = zi * twiddle[0] - zr * twiddle[1]
@@ -286,12 +304,17 @@
     modes = nn(as_one_hot(col == origin), modes).astype(bf16)
     modes = jnp.concatenate([modes[32 * h : 32 * h + 32] for h in range(16)], axis=1)
     chosen = [nt(modes, pick[pl.ds(128 * j, 128), :]) for j in range(SLOTS)]
-    flat2 = out2.reshape(DEVICES * 4, 128)
+    flat2 = out2.reshape(CHIPS * 8, 128)
+    flat_near = near2.reshape(CHIPS * 4, 128)
     for q in range(4):
         block = jnp.concatenate(
             [y[8 * q : 8 * q + 8] for y in chosen] + [jnp.zeros((32, 128), f32)], axis=0
         )
-        flat2[pl.ds(q, DEVICES, stride=4), :] = block.T
+        block = block.T
+        flat_near[pl.ds(q, CHIPS, stride=4), :] = block[CHIPS:]
+        flat2[pl.ds(core * 4 + q, CHIPS, stride=8), :] = block[:CHIPS]
+    send(near2, out2.at[:, core], 5, sibling)
+    settle(near2, 5)
     exchange(out2, in2, 1)
 
     for j in range(SLOTS):
@@ -310,9 +333,9 @@
         syn[pl.ds(16 * j, 16), :] = nn(filt[j], leg[j]).astype(bf16)
 
     col = iota((512, 512), 1)
-    by_quad = as_one_hot(iota((512, 512), 0) == col % 128 * 4 + col // 128)
+    device = 2 * (col & 63) + jnp.where((col & 127) < CHIPS, core, 1 - core)
+    by_quad = as_one_hot(iota((512, 512), 0) == device * 4 + (col >> 7))
     maps = nn(syn[...], by_quad)
-    flat3 = out3.reshape(DEVICES * 8, 128)
     for h in range(6):
         block = jnp.concatenate(
             [
@@ -321,17 +344,28 @@
                 for q in range(4)
             ],
             axis=0,
-        )
-        flat3[pl.ds(h, DEVICES, stride=8), :] = block.T
-    for h in range(6, 8):
-        flat3[pl.ds(h, DEVICES, stride=8), :] = jnp.zeros((DEVICES, 128), f32)
+        ).T
+        near3[pl.ds(CHIPS * h, CHIPS), :] = block[CHIPS:].astype(bf16)
+        stage[pl.ds(core * 8 + h, CHIPS, stride=16), :] = block[:CHIPS]
+    send(near3, got3, 6, sibling)
+    settle(near3, 6)
+    for h in range(6):
+        piece = got3[pl.ds(CHIPS * h, CHIPS), :].astype(f32)
+        stage[pl.ds(8 - core * 8 + h, CHIPS, stride=16), :] = piece
+    out3[...] = stage[...].astype(bf16).reshape(CHIPS, 16, 128)
     exchange(out3, in3, 2)
     settle(in3, 2)
 
-    flat3 = in3.reshape(DEVICES * 8, 128)
+    stage[...] = in3[...].reshape(CHIPS * 16, 128).astype(f32)
     lefts = []
     for h in range(6):
-        block = flat3[pl.ds(h, DEVICES, stride=8), :].T.astype(bf16)
+        block = jnp.concatenate(
+            [
+                stage[pl.ds(core * 8 + h, CHIPS, stride=16), :],
+                stage[pl.ds(8 - core * 8 + h, CHIPS, stride=16), :],
+            ],
+            axis=0,
+        ).T.astype(bf16)
         lefts += [block[:64], block[64:]]
     v = nn(jnp.concatenate(lefts, axis=1), pick[...])
     v = (v * jnp.where(iota((1, 2048), 1) == 0, 1.0, 2.0)).astype(bf16)
@@ -372,19 +406,10 @@
     sent(id1.at[pl.ds(0, LOCAL - 1)], 3)
     sent(id2.at[pl.ds(0, BANDS - 1)], 4)
     sent(in1.at[pl.ds(0, DEVICES - 1)], 0)
-    sent(in2.at[pl.ds(0, DEVICES - 1)], 1)
-    sent(in3.at[pl.ds(0, DEVICES - 1)], 2)
-
-
-def hand_over(kappa, potential, kappa_out, potential_out, sems):
-    copies = [
-        pltpu.make_async_copy(kappa, kappa_out, sems.at[0]),
-        pltpu.make_async_copy(potential, potential_out, sems.at[1]),
-    ]
-    for copy in copies:
-        copy.start()
-    for copy in copies:
-        copy.wait()
+    sent(near2, 5)
+    sent(near3, 6)
+    sent(in2.at[pl.ds(0, CHIPS - 1)], 1)
+    sent(in3.at[pl.ds(0, CHIPS - 1)], 2)
 
 
 def per_device(weights, offsets, counts, block_ids, m_table, legendre):
@@ -394,7 +419,7 @@
     shape = jax.ShapeDtypeStruct((NBIN, 128, 128), f32)
     kappa, potential = pl.pallas_call(
         kernel,
-        out_shape=(shape, shape),
+        out_shape=(pltpu.VMEM(shape.shape, f32),) * 2,
         in_specs=[vmem] * 5 + [hbm] * 11,
         out_specs=(vmem, vmem),
         scratch_shapes=[
@@ -402,10 +427,14 @@
             pltpu.VMEM((SLOTS, DEGREES, CYCLES), bf16),
             pltpu.VMEM((DEVICES, 32, 128), bf16),
             pltpu.VMEM((DEVICES, 32, 128), bf16),
-            pltpu.VMEM((DEVICES, 4, 128), f32),
-            pltpu.VMEM((DEVICES, 4, 128), f32),
-            pltpu.VMEM((DEVICES, 8, 128), f32),
-            pltpu.VMEM((DEVICES, 8, 128), f32),
+            pltpu.VMEM((CHIPS, 4, 128), f32),
+            pltpu.VMEM((CHIPS, 2, 4, 128), f32),
+            pltpu.VMEM((CHIPS, 2, 4, 128), f32),
+            pltpu.VMEM((CHIPS * 6, 128), bf16),
+            pltpu.VMEM((CHIPS * 6, 128), bf16),
+            pltpu.VMEM((CHIPS, 16, 128), bf16),
+            pltpu.VMEM((CHIPS, 16, 128), bf16),
+            pltpu.VMEM((CHIPS * 16, 128), f32),
             pltpu.VMEM((CAP, DEVICES), f32),
             pltpu.VMEM((LOCAL, CAP, DEVICES), f32),
             pltpu.VMEM((BANDS, 1, 128), f32),
@@ -416,8 +445,8 @@
             pltpu.VMEM((SLOTS * 16, CYCLES), bf16),
             pltpu.SemaphoreType.DMA((10,)),
             pltpu.SemaphoreType.DMA((SLOTS,)),
-            pltpu.SemaphoreType.DMA((5,)),
-            pltpu.SemaphoreType.DMA((5,)),
+            pltpu.SemaphoreType.DMA((7,)),
+            pltpu.SemaphoreType.DMA((7,)),
             pltpu.SemaphoreType.DMA((4,)),
         ],
         compiler_params=pltpu.CompilerParams(
@@ -433,14 +462,6 @@
         legendre,
         *constants,
     )
-    kappa, potential = pl.pallas_call(
-        hand_over,
-        out_shape=(shape, shape),
-        in_specs=[vmem, vmem],
-        out_specs=(hbm, hbm),
-        scratch_shapes=[pltpu.SemaphoreType.DMA((2,))],
-        name="hand_over",
-    )(kappa, potential)
     maps = [x.reshape(NBIN, 32, 4, 128).transpose(0, 2, 1, 3) for x in (kappa, potential)]
     return tuple(x.reshape(NBIN, 4, NPHI) for x in maps)
 

time: 70.5 us -> 62.8 us (0.89)
  Pallas kernels: 69.5 us -> 60.6 us
  local copies, waits for them, and re-layouts: 0 us -> 1.41 us
    pallas_call x2 -> x1, Pallas kernels: 69.5 us -> 60.6 us  [per_device(): pl.pallas_call(kernel, out_shape=(pltpu.VMEM(shape.shape, f32),) * 2, in_...]
    unnamed x0 -> x2, local copies, waits for them, and re-layouts: none -> 1.41 us
where the time goes in v3:
time: 62.8 us; the launch traced here: 62.7 us
  Pallas kernels  60.6 us (96%)
  local copies, waits for them, and re-layouts  1.41 us (2%)
  between operations  0.64 us (1%)
    pallas_call x1, Pallas kernels, per_device(): pl.pallas_call(kernel, out_shape=(pltpu.VMEM(shape.shape, f32),) * 2, in_...  60.6 us
    unnamed x2, local copies, waits for them, and re-layouts  1.41 us

profile of v3, /device:TPU:1, one launch (start us, length us, event | category | flops | bytes accessed | tf_op | source)
XLA Modules:
  0.0 62.7 jit_solution(9135169802124269900)
XLA Ops:
  0.6 60.6 %deposit_filter.1 = (f32[4,128,128]{2,1,0:T(8,128)S(1)}, f32[4,128,128]{2,1,0:T(8,128)S(1)}) custom-call(bf16[128,32,128]{2,1,0:T(8,128)(2,1)} %bitcast.17, s32[128,8,128]{2,1,0:T(8,128)} %bitcast.18, s32[8,128]{1,0:T(8,128)} %bitcast.19, s32[1,128]{1,0:T(1,128)} %refs_3_.1, s32[1536]{0:T(1024)} %refs_4_.1, bf16[12,1664,512]{2,1,0:T(8,128)(2,1)} %refs_5_.1, ...), custom_call_target="tpu_custom_call" | custom-call | tf_op jit(solution)/shard_map/deposit_filter/pallas_call | solution.py:420
  61.3 0.7 %copy.22 = f32[4,4,4096]{2,1,0:T(4,128)} copy(f32[4,4,4096]{2,1,0:T(4,128)S(1)} %bitcast.16) | data formatting | bytes 524288
  62.0 0.7 %copy.23 = f32[4,4,4096]{2,1,0:T(4,128)} copy(f32[4,4,4096]{2,1,0:T(4,128)S(1)} %bitcast.15) | data formatting | bytes 524288

commit v4 on v3

--- a/solution.py
+++ b/solution.py
@@ -21,7 +21,7 @@
 PART = 32
 BATCH = 8
 STRIDE = 27
-EARLY = 16
+EARLY = 24
 MESH_IDS = pl.DeviceIdType.MESH
 bf16 = jnp.bfloat16
 f32 = jnp.float32
@@ -104,14 +104,14 @@
 
 def kernel(*refs):
     (
-        w_ref, off_ref, blocks_ref, counts_ref, orders_ref, leg_ref, *constants,
+        w_hbm, off_hbm, blocks_ref, counts_ref, orders_ref, leg_ref, *constants,
     ) = refs[:16]
     kappa_ref, potential_ref = refs[16:18]
     held = refs[18:28]
     first_h, first_l, twiddle, second_h, second_l, half, back, unwind, last_h, last_l = held
     (
         leg, out1, in1, near2, out2, in2, near3, got3, out3, in3, stage, id0, id1, idx, id2, sel, pick, filt, syn,
-        const_sem, leg_sem, send_sem, recv_sem, part_sem,
+        w_ref, off_ref, order, doubled, by_quad, gain, load_sem, const_sem, leg_sem, send_sem, recv_sem, part_sem,
     ) = refs[28:]
     band = lax.axis_index("blk")
     local = lax.axis_index("ma")
@@ -119,6 +119,16 @@
     core = lax.rem(local, 2)
     chip = me // 2
     sibling = (band, local + 1 - 2 * core)
+
+    loads = []
+    for k in range(4):
+        rows = pl.ds(32 * k, 32)
+        loads.append(pltpu.make_async_copy(w_hbm.at[rows], w_ref.at[rows], load_sem.at[2 * k]))
+        loads.append(
+            pltpu.make_async_copy(off_hbm.at[rows], off_ref.at[rows], load_sem.at[2 * k + 1])
+        )
+    for load in loads:
+        load.start()
 
     barrier = pltpu.get_barrier_semaphore()
 
@@ -195,6 +205,8 @@
 
     live = iota((CAP, DEVICES), 0) < counts_ref[...]
     id0[...] = jnp.where(live, blocks_ref[...], -1).astype(f32)
+    for load in loads:
+        load.wait()
     lax.fori_loop(0, EARLY, deposit, 0, unroll=4)
     pl.semaphore_wait(barrier, DEVICES - 1)
 
@@ -255,6 +267,21 @@
     label = jnp.where(m2 < 48, lane // 128 * 2 + lane // 64 % 2 + 32 * m2, -1).astype(f32)
     for j in range(SLOTS):
         pick[pl.ds(128 * j, 128), :] = as_one_hot(orders[:, j : j + 1] == label)
+
+    row = iota((512, 1), 0)
+    origin = ((row >> 2) & 1) * 256 + (row & 3) * 64 + (row >> 5) * 4 + ((row >> 3) & 3)
+    order[...] = as_one_hot(iota((512, 512), 1) == origin)
+    row = iota((192, 1), 0)
+    origin = (row >> 4) * 8 + ((row >> 3) & 1) * 4 + (row & 3)
+    doubled[...] = as_one_hot(iota((192, 128), 1) == origin)
+    col = iota((1, 512), 1)
+    device = 2 * (col & 63) + jnp.where((col & 127) < CHIPS, core, 1 - core)
+    by_quad[...] = as_one_hot(iota((512, 512), 0) == device * 4 + (col >> 7))
+    degree = iota((16, DEGREES), 1).astype(f32)
+    filter_gain = jnp.where(
+        degree > 0.5, -20000.0 / jnp.maximum(degree * (degree + 1.0), 1.0), 0.0
+    )
+    gain[...] = jnp.where(((iota((16, DEGREES), 0) >> 2) & 1) == 1, filter_gain, 1.0)
 
     settle(id2, 4)
     at = iota((128, 4096), 1)
@@ -299,9 +326,7 @@
     c = jnp.where(odd, half[0:1, :], 1.0)
     s = jnp.where(odd, half[1:2, :], 0.0)
     modes = jnp.concatenate([xr * c + xi * s, xi * c - xr * s], axis=0).astype(bf16)
-    row, col = iota((512, 512), 0), iota((512, 512), 1)
-    origin = row // 4 % 2 * 256 + row % 4 * 64 + row // 32 * 4 + row // 8 % 4
-    modes = nn(as_one_hot(col == origin), modes).astype(bf16)
+    modes = nn(order[...], modes).astype(bf16)
     modes = jnp.concatenate([modes[32 * h : 32 * h + 32] for h in range(16)], axis=1)
     chosen = [nt(modes, pick[pl.ds(128 * j, 128), :]) for j in range(SLOTS)]
     flat2 = out2.reshape(CHIPS * 8, 128)
@@ -319,23 +344,15 @@
 
     for j in range(SLOTS):
         pltpu.make_async_copy(leg_ref.at[j], leg.at[j], leg_sem.at[j]).wait()
-    degree = iota((16, DEGREES), 1).astype(f32)
-    gain = jnp.where(degree > 0.5, -20000.0 / jnp.maximum(degree * (degree + 1.0), 1.0), 0.0)
-    gain = jnp.where(iota((16, DEGREES), 0) // 4 % 2 == 1, gain, 1.0)
-    row = iota((192, 128), 0)
-    doubled = as_one_hot(iota((192, 128), 1) == row // 16 * 8 + row // 8 % 2 * 4 + row % 4)
-
     settle(in2, 1)
-    mode_rows = nt(doubled, in2[...].reshape(CYCLES, 128).astype(bf16)).astype(bf16)
-    for j in range(SLOTS):
-        filt[j] = (nt(mode_rows[16 * j : 16 * j + 16], leg[j]) * gain).astype(bf16)
-    for j in range(SLOTS):
-        syn[pl.ds(16 * j, 16), :] = nn(filt[j], leg[j]).astype(bf16)
-
-    col = iota((512, 512), 1)
-    device = 2 * (col & 63) + jnp.where((col & 127) < CHIPS, core, 1 - core)
-    by_quad = as_one_hot(iota((512, 512), 0) == device * 4 + (col >> 7))
-    maps = nn(syn[...], by_quad)
+    mode_rows = nt(doubled[...], in2[...].reshape(CYCLES, 128).astype(bf16)).astype(bf16)
+    for j in range(SLOTS + 1):
+        if j < SLOTS:
+            filt[j] = (nt(mode_rows[16 * j : 16 * j + 16], leg[j]) * gain[...]).astype(bf16)
+        if j > 0:
+            syn[pl.ds(16 * j - 16, 16), :] = nn(filt[j - 1], leg[j - 1]).astype(bf16)
+
+    maps = nn(syn[...], by_quad[...])
     for h in range(6):
         block = jnp.concatenate(
             [
@@ -420,7 +437,7 @@
     kappa, potential = pl.pallas_call(
         kernel,
         out_shape=(pltpu.VMEM(shape.shape, f32),) * 2,
-        in_specs=[vmem] * 5 + [hbm] * 11,
+        in_specs=[hbm] * 2 + [vmem] * 3 + [hbm] * 11,
         out_specs=(vmem, vmem),
         scratch_shapes=[
             *[pltpu.VMEM(t.shape, t.dtype) for t in constants],
@@ -443,6 +460,13 @@
             pltpu.VMEM((SLOTS * 128, 2048), bf16),
             pltpu.VMEM((SLOTS, 16, DEGREES), bf16),
             pltpu.VMEM((SLOTS * 16, CYCLES), bf16),
+            pltpu.VMEM((DEVICES, CAP * NBIN, 128), bf16),
+            pltpu.VMEM((DEVICES, CAP, 128), jnp.int32),
+            pltpu.VMEM((512, 512), bf16),
+            pltpu.VMEM((SLOTS * 16, 128), bf16),
+            pltpu.VMEM((512, 512), bf16),
+            pltpu.VMEM((16, DEGREES), f32),
+            pltpu.SemaphoreType.DMA((8,)),
             pltpu.SemaphoreType.DMA((10,)),
             pltpu.SemaphoreType.DMA((SLOTS,)),
             pltpu.SemaphoreType.DMA((7,)),

time: 62.8 us -> 62.1 us (0.989)
  Pallas kernels: 60.6 us -> 59.9 us
    pallas_call x1, Pallas kernels: 60.6 us -> 59.9 us  [per_device(): pl.pallas_call(kernel, out_shape=(pltpu.VMEM(shape.shape, f32),) * 2, in_...]
where the time goes in v4:
time: 62.1 us; the launch traced here: 62 us
  Pallas kernels  59.9 us (96%)
  local copies, waits for them, and re-layouts  1.41 us (2%)
  between operations  0.64 us (1%)
    pallas_call x1, Pallas kernels, per_device(): pl.pallas_call(kernel, out_shape=(pltpu.VMEM(shape.shape, f32),) * 2, in_...  59.9 us
    unnamed x2, local copies, waits for them, and re-layouts  1.41 us

profile of v4, /device:TPU:1, one launch (start us, length us, event | category | flops | bytes accessed | tf_op | source)
XLA Modules:
  0.0 62.0 jit_solution(17867065141258891141)
XLA Ops:
  0.6 59.9 %deposit_filter.1 = (f32[4,128,128]{2,1,0:T(8,128)S(1)}, f32[4,128,128]{2,1,0:T(8,128)S(1)}) custom-call(bf16[128,32,128]{2,1,0:T(8,128)(2,1)} %bitcast.17, s32[128,8,128]{2,1,0:T(8,128)} %bitcast.18, s32[8,128]{1,0:T(8,128)} %bitcast.19, s32[1,128]{1,0:T(1,128)} %refs_3_.1, s32[1536]{0:T(1024)} %refs_4_.1, bf16[12,1664,512]{2,1,0:T(8,128)(2,1)} %refs_5_.1, ...), custom_call_target="tpu_custom_call" | custom-call | tf_op jit(solution)/shard_map/deposit_filter/pallas_call | solution.py:437
  60.5 0.7 %copy.22 = f32[4,4,4096]{2,1,0:T(4,128)} copy(f32[4,4,4096]{2,1,0:T(4,128)S(1)} %bitcast.16) | data formatting | bytes 524288
  61.2 0.7 %copy.23 = f32[4,4,4096]{2,1,0:T(4,128)} copy(f32[4,4,4096]{2,1,0:T(4,128)S(1)} %bitcast.15) | data formatting | bytes 524288

commit v5 on v4

--- a/solution.py
+++ b/solution.py
@@ -331,14 +331,17 @@
     chosen = [nt(modes, pick[pl.ds(128 * j, 128), :]) for j in range(SLOTS)]
     flat2 = out2.reshape(CHIPS * 8, 128)
     flat_near = near2.reshape(CHIPS * 4, 128)
+    own = []
     for q in range(4):
         block = jnp.concatenate(
             [y[8 * q : 8 * q + 8] for y in chosen] + [jnp.zeros((32, 128), f32)], axis=0
         )
         block = block.T
         flat_near[pl.ds(q, CHIPS, stride=4), :] = block[CHIPS:]
-        flat2[pl.ds(core * 4 + q, CHIPS, stride=8), :] = block[:CHIPS]
+        own.append(block[:CHIPS])
     send(near2, out2.at[:, core], 5, sibling)
+    for q in range(4):
+        flat2[pl.ds(core * 4 + q, CHIPS, stride=8), :] = own[q]
     settle(near2, 5)
     exchange(out2, in2, 1)
 
@@ -353,6 +356,7 @@
             syn[pl.ds(16 * j - 16, 16), :] = nn(filt[j - 1], leg[j - 1]).astype(bf16)
 
     maps = nn(syn[...], by_quad[...])
+    own = []
     for h in range(6):
         block = jnp.concatenate(
             [
@@ -363,8 +367,10 @@
             axis=0,
         ).T
         near3[pl.ds(CHIPS * h, CHIPS), :] = block[CHIPS:].astype(bf16)
-        stage[pl.ds(core * 8 + h, CHIPS, stride=16), :] = block[:CHIPS]
+        own.append(block[:CHIPS])
     send(near3, got3, 6, sibling)
+    for h in range(6):
+        stage[pl.ds(core * 8 + h, CHIPS, stride=16), :] = own[h]
     settle(near3, 6)
     for h in range(6):
         piece = got3[pl.ds(CHIPS * h, CHIPS), :].astype(f32)

time: 62.1 us -> 62.1 us (level)
  no operation moved by 1% of the time
where the time goes in v5:
time: 62.1 us; the launch traced here: 61.9 us
  Pallas kernels  59.9 us (96%)
  local copies, waits for them, and re-layouts  1.41 us (2%)
  between operations  0.64 us (1%)
    pallas_call x1, Pallas kernels, per_device(): pl.pallas_call(kernel, out_shape=(pltpu.VMEM(shape.shape, f32),) * 2, in_...  59.9 us
    unnamed x2, local copies, waits for them, and re-layouts  1.41 us

profile of v5, /device:TPU:1, one launch (start us, length us, event | category | flops | bytes accessed | tf_op | source)
XLA Modules:
  0.0 61.9 jit_solution(17401198527966108751)
XLA Ops:
  0.6 59.9 %deposit_filter.1 = (f32[4,128,128]{2,1,0:T(8,128)S(1)}, f32[4,128,128]{2,1,0:T(8,128)S(1)}) custom-call(bf16[128,32,128]{2,1,0:T(8,128)(2,1)} %bitcast.17, s32[128,8,128]{2,1,0:T(8,128)} %bitcast.18, s32[8,128]{1,0:T(8,128)} %bitcast.19, s32[1,128]{1,0:T(1,128)} %refs_3_.1, s32[1536]{0:T(1024)} %refs_4_.1, bf16[12,1664,512]{2,1,0:T(8,128)(2,1)} %refs_5_.1, ...), custom_call_target="tpu_custom_call" | custom-call | tf_op jit(solution)/shard_map/deposit_filter/pallas_call | solution.py:443
  60.5 0.7 %copy.22 = f32[4,4,4096]{2,1,0:T(4,128)} copy(f32[4,4,4096]{2,1,0:T(4,128)S(1)} %bitcast.16) | data formatting | bytes 524288
  61.2 0.7 %copy.23 = f32[4,4,4096]{2,1,0:T(4,128)} copy(f32[4,4,4096]{2,1,0:T(4,128)S(1)} %bitcast.15) | data formatting | bytes 524288
